TPU v7x, 128 devices: a whole 4x4x4 slice. The times are simulated.
128 devices in a mesh: dp: 4 (over y_hi, core), ctx: 32 (over y_lo, z, x).
Axes of the slice: x: 4, y: 4 (y_hi: 2, y_lo: 2; y = y_hi * 2 + y_lo), z: 4, core: 2. Of those that a mesh axis runs over, the one named last changes fastest.
Arguments:
- trunk_input: bfloat16 [4, 8192, 768], P('dp', 'ctx'), may hold values from -6 to 6
- tokens: int32 [4, 8192], P('dp', 'ctx'), may hold values from 0 to 3
- token_table: float32 [4, 768], replicated, may hold values from -3 to 3
- conv_weight: bfloat16 [2, 3, 768, 384], replicated, may hold values from -0.125 to 0.125
- out_weight: bfloat16 [2, 384, 768], replicated, may hold values from -0.3125 to 0.3125
- norm_gain: float32 [2, 768], replicated, may hold values from 0.1 to 1.9
- mid_gain: float32 [2, 384], replicated, may hold values from 0.1 to 1.9
- strand_perm: int32 [768], replicated, may hold values from 0 to 767, each once
- dilation: int32 [2], replicated, may hold values from 1 to 64, as said below
- out_cotangent: bfloat16 [4, 8192, 768], P('dp', 'ctx'), may hold values from -6 to 6
Outputs:
- block_output: bfloat16 [4, 8192, 768], P('dp', 'ctx')
- trunk_grad: bfloat16 [4, 8192, 768], P('dp', 'ctx')
- table_grad: float32 [4, 768], replicated
- conv_grad: float32 [2, 3, 768, 384], replicated
- out_weight_grad: float32 [2, 384, 768], replicated
- norm_gain_grad: float32 [2, 768], replicated
- mid_gain_grad: float32 [2, 384], replicated
Inputs may be any that keep to these rules, and one draw needn't show every extreme that they name: Each block's dilation lies in 1 .. 64, and some block has exactly 64. `strand_perm`: each channel index appears once.
All inputs are finite; a program needn't handle non-finite values.
Results may differ from a plain program's by a relative error of at most 0.014.
Values may be sent and summed in bfloat16 or wider, within the bound.
A program may use at most 128 MiB of HBM per device.

v0:
```python
import jax
import jax.numpy as jnp
from jax import lax
from jax.experimental import pallas as pl
from jax.experimental.pallas import tpu as pltpu
from jax.sharding import PartitionSpec as P

LAYERS = 2
DMAX = 64

MESH = pl.DeviceIdType.MESH
GROWS = 3072
HALF = 1536
QUARTER = 384
EIGHTH = 96
SMALL = 16
LANES = 384


def place(core, y, z, x):
    return (lax.div(y, 2) * 2 + core, (lax.rem(y, 2) * 4 + z) * 4 + x)


def coordinates():
    dp = lax.axis_index("dp")
    ctx = lax.axis_index("ctx")
    y = lax.div(dp, 2) * 2 + lax.div(ctx, 16)
    return (lax.rem(dp, 2), y, lax.rem(lax.div(ctx, 4), 4), lax.rem(ctx, 4))


def ring_peer(spot, axis, distance):
    moved = list(spot)
    moved[axis] = lax.rem(spot[axis] + distance, 4)
    return place(*moved)


def core_peer(spot):
    return place(1 - spot[0], *spot[1:])


ORDERS = ((3, 1, 2), (1, 2, 3), (2, 3, 1))


class Copies:
    def __init__(self, send, recv):
        self.send, self.recv, self.open = send, recv, []

    def start(self, index, source, target, device):
        copy = pltpu.make_async_remote_copy(
            src_ref=source, dst_ref=target, send_sem=self.send.at[index],
            recv_sem=self.recv.at[index], device_id=device, device_id_type=MESH)
        copy.start()
        return copy


class Total:
    def __init__(self, spot, grads, result, core_in, sums0, in_a, sums1, in_b, sums2, in_c, send, recv):
        self.spot, self.grads, self.result = spot, grads, result
        self.core_in, self.sums0, self.in_a, self.sums1 = core_in, sums0, in_a, sums1
        self.in_b, self.sums2, self.in_c = in_b, sums2, in_c
        self.copies = Copies(send, recv)
        self.base = spot[0] * HALF

    def lanes(self, third):
        return pl.ds(third * 128, 128)

    def core_start(self):
        other = (1 - self.spot[0]) * HALF
        self.core = self.copies.start(0, self.grads.at[pl.ds(other, HALF)], self.core_in, core_peer(self.spot))

    def core_finish(self):
        self.core.wait()

        def body(step, carry):
            rows = pl.ds(pl.multiple_of(step * QUARTER, 32), QUARTER)
            mine = pl.ds(pl.multiple_of(self.base + step * QUARTER, 32), QUARTER)
            self.sums0[rows] = (self.grads[mine].astype(jnp.float32) + self.core_in[rows].astype(jnp.float32)).astype(jnp.bfloat16)
            return carry

        lax.fori_loop(0, 4, body, 0)

    def a_start(self):
        self.a = []
        for third, order in enumerate(ORDERS):
            for distance in (2, 1, 3):
                chunk = lax.rem(self.spot[order[0]] + distance, 4)
                self.a.append(self.copies.start(
                    1 + third * 3 + distance - 1,
                    self.sums0.at[pl.ds(chunk * QUARTER, QUARTER), self.lanes(third)],
                    self.in_a.at[third, distance - 1], ring_peer(self.spot, order[0], distance)))

    def a_finish(self):
        for copy in self.a:
            copy.wait()
        for third, order in enumerate(ORDERS):
            mine = pl.ds(pl.multiple_of(self.spot[order[0]] * QUARTER, 32), QUARTER)
            total = self.sums0[mine, self.lanes(third)].astype(jnp.float32)
            for slot in range(3):
                total = total + self.in_a[third, slot].astype(jnp.float32)
            self.sums1[third] = total.astype(jnp.bfloat16)

    def b_start(self):
        self.b = []
        for third, order in enumerate(ORDERS):
            for distance in (2, 1, 3):
                chunk = lax.rem(self.spot[order[1]] + distance, 4)
                self.b.append(self.copies.start(
                    10 + third * 3 + distance - 1,
                    self.sums1.at[third, pl.ds(chunk * EIGHTH, EIGHTH)],
                    self.in_b.at[third, distance - 1], ring_peer(self.spot, order[1], distance)))

    def b_finish(self):
        for copy in self.b:
            copy.wait()
        for third, order in enumerate(ORDERS):
            mine = pl.ds(pl.multiple_of(self.spot[order[1]] * EIGHTH, 32), EIGHTH)
            total = self.sums1[third, mine].astype(jnp.float32)
            for slot in range(3):
                total = total + self.in_b[third, slot].astype(jnp.float32)
            self.sums2[third] = total.astype(jnp.bfloat16)

    def c_start(self):
        self.c = []
        for third, order in enumerate(ORDERS):
            for distance in (2, 1, 3):
                self.c.append(self.copies.start(
                    19 + third * 3 + distance - 1, self.sums2.at[third],
                    self.in_c.at[third, self.spot[order[2]]], ring_peer(self.spot, order[2], distance)))
            self.in_c[third, self.spot[order[2]]] = self.sums2[third]

    def rows_of(self, third):
        order = ORDERS[third]
        quarter = self.base + self.spot[order[0]] * QUARTER
        return quarter, quarter + self.spot[order[1]] * EIGHTH

    def c_finish(self):
        for copy in self.c:
            copy.wait()
        for third in range(3):
            total = self.in_c[third, 0].astype(jnp.float32)
            for slot in range(1, 4):
                total = total + self.in_c[third, slot].astype(jnp.float32)
            _, eighth = self.rows_of(third)
            self.result[pl.ds(pl.multiple_of(eighth, 32), EIGHTH), self.lanes(third)] = total.astype(jnp.bfloat16)

    def gather_start(self, which):
        copies = []
        for third, order in enumerate(ORDERS):
            quarter, eighth = self.rows_of(third)
            rows = pl.ds(eighth, EIGHTH) if which else pl.ds(quarter, QUARTER)
            piece = self.result.at[rows, self.lanes(third)]
            for distance in (2, 1, 3):
                copies.append(self.copies.start(
                    28 + which * 9 + third * 3 + distance - 1, piece, piece, ring_peer(self.spot, order[which], distance)))
        return copies

    def last_start(self):
        piece = self.result.at[pl.ds(self.base, HALF)]
        return self.copies.start(46, piece, piece, core_peer(self.spot))


TOTAL_COPIES = 47


def total_scratch():
    return [
        pltpu.VMEM((HALF, LANES), jnp.bfloat16),
        pltpu.VMEM((HALF, LANES), jnp.bfloat16),
        pltpu.VMEM((3, 3, QUARTER, 128), jnp.bfloat16),
        pltpu.VMEM((3, QUARTER, 128), jnp.bfloat16),
        pltpu.VMEM((3, 3, EIGHTH, 128), jnp.bfloat16),
        pltpu.VMEM((3, EIGHTH, 128), jnp.bfloat16),
        pltpu.VMEM((3, 4, EIGHTH, 128), jnp.bfloat16),
        pltpu.SemaphoreType.DMA((TOTAL_COPIES,)),
        pltpu.SemaphoreType.DMA((TOTAL_COPIES,)),
    ]


class Small:
    def __init__(self, spot, value, core_in, ring_in, send, recv):
        self.spot, self.value, self.core_in, self.ring_in = spot, value, core_in, ring_in
        self.copies = Copies(send, recv)

    def core_start(self):
        self.core = self.copies.start(0, self.value, self.core_in, core_peer(self.spot))

    def core_finish(self):
        self.core.wait()
        own = self.spot[3]
        self.ring_in[0, own] = self.value[...] + self.core_in[...]

    def ring_start(self, stage):
        axis = (3, 1, 2)[stage]
        own = self.spot[axis]
        self.ring = [
            self.copies.start(1 + stage * 3 + distance - 1, self.ring_in.at[stage, own], self.ring_in.at[stage, own],
                              ring_peer(self.spot, axis, distance)) for distance in (2, 1, 3)]

    def ring_finish(self, stage):
        for copy in self.ring:
            copy.wait()
        total = self.ring_in[stage, 0] + self.ring_in[stage, 1] + self.ring_in[stage, 2] + self.ring_in[stage, 3]
        if stage < 2:
            self.ring_in[stage + 1, self.spot[(3, 1, 2)[stage + 1]]] = total
        return total


def small_scratch():
    return [
        pltpu.VMEM((SMALL, LANES), jnp.float32),
        pltpu.VMEM((3, 4, SMALL, LANES), jnp.float32),
        pltpu.SemaphoreType.DMA((10,)),
        pltpu.SemaphoreType.DMA((10,)),
    ]


def greet(spot, extra=()):
    barrier = pltpu.get_barrier_semaphore()
    peers = [core_peer(spot)] + [ring_peer(spot, axis, distance) for axis in (1, 2, 3) for distance in (1, 2, 3)]
    peers += list(extra)
    for peer in peers:
        pl.semaphore_signal(barrier, inc=1, device_id=peer, device_id_type=MESH)
    pl.semaphore_wait(barrier, len(peers))


epsilon = 1e-05
OWN = 256
WIDE = OWN + 2 * DMAX
CH = 768
MID = 384
TILE = 32
BF = jnp.bfloat16
F32 = jnp.float32


def dot(left, right):
    return jnp.dot(left, right, preferred_element_type=F32)


def dot_t(left, right):
    return lax.dot_general(left, right, (((1,), (1,)), ((), ())), preferred_element_type=F32)


def dot_rows(left, right):
    return lax.dot_general(left, right, (((0,), (0,)), ((), ())), preferred_element_type=F32)


def strand(s, width=CH):
    return pl.ds(s * width, width)


def loop(count, body):
    def step(index, carry):
        body(index)
        return carry

    lax.fori_loop(0, count, step, 0)


def tile_at(index, base=0, size=TILE):
    return pl.ds(pl.multiple_of(base + index * size, size), size)


def standard(values):
    centre = jnp.mean(values, axis=-1, keepdims=True)
    shifted = values - centre
    scale = lax.rsqrt(jnp.mean(shifted * shifted, axis=-1, keepdims=True) + epsilon)
    return shifted * scale, centre, scale


def gelu_pair(z):
    below = 0.5 + 0.5 * lax.erf(z * 0.7071067811865476)
    return z * below, below + z * (0.3989422804014327 * jnp.exp(-0.5 * z * z))


def norm_back(dz, hat, scale, gain):
    dhat = dz * gain
    return scale * (
        dhat - jnp.mean(dhat, axis=-1, keepdims=True) - hat * jnp.mean(dhat * hat, axis=-1, keepdims=True)
    )


def fold(values):
    return values.reshape(TILE // 8, 8, values.shape[-1]).sum(axis=0)


def step_kernel(
    dilation, trunk, tokens, table, norm_gain, mid_gain, perm, cotangent, conv_hbm, out_hbm,
    block_out, trunk_grad, result, small_out,
    conv_w, out_w, matrix, move, hidden, relabelled, u_pad, u_low, u_high, hat, slope, scale, mid,
    mid_hat, mid_slope, mid_scale, q, wide, back, rounded, e, dm_pad, dm_low, dm_high, grad, gain_acc, mid_acc,
    weight_sem, halo_send, halo_recv, grads, *scratch,
):
    spot = coordinates()
    dp = lax.axis_index("dp")
    ctx = lax.axis_index("ctx")
    left = (dp, lax.rem(ctx + 31, 32))
    right = (dp, lax.rem(ctx + 1, 32))
    first_bin = jnp.where(ctx == 0, DMAX, 0)
    end_bin = jnp.where(ctx == 31, DMAX + OWN, WIDE)
    weights = [
        pltpu.make_async_copy(conv_hbm, conv_w, weight_sem.at[0]),
        pltpu.make_async_copy(out_hbm, out_w, weight_sem.at[1]),
    ]
    for copy in weights:
        copy.start()
    each = len(total_scratch())
    totals = [Total(spot, grads.at[b], result.at[b], *scratch[b * each:(b + 1) * each]) for b in range(LAYERS)]
    small = Small(spot, *scratch[2 * each:])
    halos = Copies(halo_send, halo_recv)

    def trade(index, mine):
        return [
            halos.start(2 * index, mine.at[pl.ds(DMAX, DMAX)], mine.at[pl.ds(DMAX + OWN, DMAX)], left),
            halos.start(2 * index + 1, mine.at[pl.ds(OWN, DMAX)], mine.at[pl.ds(0, DMAX)], right),
        ]

    one_hot = (tokens[...] == lax.broadcasted_iota(jnp.int32, (8, OWN), 0)).astype(F32)
    added = lax.dot_general(one_hot, table[...], (((0,), (0,)), ((), ())), precision=lax.Precision.HIGHEST, preferred_element_type=F32)
    hidden[0, pl.ds(DMAX, OWN)] = (trunk[...].astype(F32) + added).astype(BF)
    greet(spot, (left, right))
    pending = trade(0, hidden.at[0])

    def fill_matrix(index):
        rows = tile_at(index)
        channel = lax.broadcasted_iota(jnp.int32, (TILE, CH), 0) + index * TILE
        matrix[rows] = jnp.where(channel == perm[...], 1.0, 0.0).astype(BF)

    loop(CH // TILE, fill_matrix)
    bin_from = lax.broadcasted_iota(jnp.int32, (OWN, WIDE), 1)
    bin_to = lax.broadcasted_iota(jnp.int32, (OWN, WIDE), 0) + DMAX
    inside = (bin_from >= first_bin) & (bin_from < end_bin)
    for b in range(LAYERS):
        for way in range(2):
            at = bin_to + (2 * way - 1) * dilation[b]
            move[b, way] = jnp.where(inside & (bin_from == at), 1.0, 0.0).astype(BF)
    e[pl.ds(0, OWN)] = (0.5 * cotangent[...].astype(F32)).astype(BF)

    for b in range(LAYERS):
        gain = norm_gain[pl.ds(b, 1)]
        mid_s = mid_gain[pl.ds(b, 1)]

        def front(rows, own):
            x = hidden[b, rows].astype(F32)
            hat_f, centre, inv = standard(x)
            hat_r = (relabelled[rows] - centre) * inv
            for s, normed in enumerate((hat_f, hat_r)):
                u, du = gelu_pair(normed * gain)
                u_pad[b, rows, strand(s)] = u.astype(BF)
                if own is not None:
                    hat[b, s, own] = normed
                    slope[b, s, own] = du
            if own is not None:
                scale[b, own] = jnp.broadcast_to(inv, (TILE, 128))

        relabelled[pl.ds(DMAX, OWN)] = dot(hidden[b, pl.ds(DMAX, OWN)], matrix[...])
        loop(OWN // TILE, lambda i: front(tile_at(i, DMAX), tile_at(i)))
        if b == 0:
            for copy in weights:
                copy.wait()
        for s in range(2):
            mid[s] = dot(u_pad[b, pl.ds(DMAX, OWN), strand(s)], conv_w[b, 1])
        for copy in pending:
            copy.wait()
        for base in (0, DMAX + OWN):
            relabelled[pl.ds(base, DMAX)] = dot(hidden[b, pl.ds(base, DMAX)], matrix[...])
            loop(DMAX // TILE, lambda i: front(tile_at(i, base), None))

        for s in range(2):
            u_low[s] = dot(move[b, s], u_pad[b, :, strand(s)]).astype(BF)
            u_high[s] = dot(move[b, 1 - s], u_pad[b, :, strand(s)]).astype(BF)
        for s in range(2):
            mid[s] += dot(u_low[s], conv_w[b, 0]) + dot(u_high[s], conv_w[b, 2])

        def middle(i):
            rows = tile_at(i)
            for s in range(2):
                normed, _, inv = standard(mid[s, rows])
                value, derivative = gelu_pair(normed * mid_s)
                q[b, s, rows] = value.astype(BF)
                mid_hat[b, s, rows] = normed
                mid_slope[b, s, rows] = derivative
                mid_scale[b, s, rows] = jnp.broadcast_to(inv, (TILE, 128))

        loop(OWN // TILE, middle)
        rounded[...] = dot(q[b, 1], out_w[b]).astype(BF)
        wide[0] = dot(q[b, 0], out_w[b])
        back[...] = dot_t(rounded[...], matrix[...])

        def join(i):
            rows = tile_at(i)
            total = wide[0, rows].astype(BF).astype(F32) + back[rows]
            following = (hidden[b, tile_at(i, DMAX)].astype(F32) + 0.5 * total).astype(BF)
            if b + 1 < LAYERS:
                hidden[b + 1, tile_at(i, DMAX)] = following
            else:
                block_out[rows] = following

        loop(OWN // TILE, join)
        if b + 1 < LAYERS:
            pending = trade(b + 1, hidden.at[b + 1])

    grad[...] = cotangent[...]
    gain_acc[...] = jnp.zeros_like(gain_acc)
    mid_acc[...] = jnp.zeros_like(mid_acc)
    for b in (1, 0):
        gain = norm_gain[pl.ds(b, 1)]
        mid_s = mid_gain[pl.ds(b, 1)]
        sums = grads.at[b]
        if b == 0:
            e[pl.ds(0, OWN)] = (0.5 * grad[...].astype(F32)).astype(BF)
        e[pl.ds(OWN, OWN)] = dot(e[pl.ds(0, OWN)], matrix[...]).astype(BF)
        for s in range(2):
            mid[s] = dot_t(e[pl.ds(s * OWN, OWN)], out_w[b])

        def middle_back(i):
            rows = tile_at(i)
            total = jnp.zeros((8, MID), F32)
            for s in range(2):
                dz = mid[s, rows] * mid_slope[b, s, rows]
                normed = mid_hat[b, s, rows]
                total = total + fold(dz * normed)
                dm = norm_back(dz, normed, mid_scale[b, s, rows, 0:1], mid_s)
                dm_pad[b, tile_at(i, DMAX), strand(s, MID)] = dm.astype(BF)
            mid_acc[b] += total

        loop(OWN // TILE, middle_back)
        pending = trade(LAYERS + b, dm_pad.at[b])
        if b == 0:
            totals[1].a_finish()
            totals[1].b_start()
        q_all = q[b].reshape(2 * OWN, MID)
        out_grad = dot_rows(q_all, e[...])
        sums[pl.ds(2304, MID)] = out_grad[:, :MID].astype(BF)
        sums[pl.ds(2688, MID)] = out_grad[:, MID:].astype(BF)
        own = pl.ds(DMAX, OWN)
        u_all = jnp.concatenate([u_pad[b, own, strand(s)] for s in range(2)], axis=0)
        dm_all = jnp.concatenate([dm_pad[b, own, strand(s, MID)] for s in range(2)], axis=0)
        sums[pl.ds(CH, CH)] = dot_rows(u_all, dm_all).astype(BF)
        for s in range(2):
            wide[s] = dot_t(dm_pad[b, own, strand(s, MID)], conv_w[b, 1])
        for copy in pending:
            copy.wait()
        for s in range(2):
            dm_low[s] = dot(move[b, 1 - s], dm_pad[b, :, strand(s, MID)]).astype(BF)
            dm_high[s] = dot(move[b, s], dm_pad[b, :, strand(s, MID)]).astype(BF)
        sums[pl.ds(0, CH)] = dot_rows(u_all, dm_low[...].reshape(2 * OWN, MID)).astype(BF)
        sums[pl.ds(2 * CH, CH)] = dot_rows(u_all, dm_high[...].reshape(2 * OWN, MID)).astype(BF)
        totals[b].core_start()
        if b == 0:
            totals[1].b_finish()
            totals[1].c_start()
        for s in range(2):
            wide[s] += dot_t(dm_low[s], conv_w[b, 0]) + dot_t(dm_high[s], conv_w[b, 2])

        def front_back(i):
            rows = tile_at(i)
            total = jnp.zeros((8, CH), F32)
            for s in range(2):
                dz = wide[s, rows] * slope[b, s, rows]
                normed = hat[b, s, rows]
                total = total + fold(dz * normed)
                dx = norm_back(dz, normed, scale[b, rows, 0:1], gain)
                if s == 0:
                    wide[0, rows] = dx
                else:
                    rounded[rows] = dx.astype(BF)
            gain_acc[b] += total

        loop(OWN // TILE, front_back)
        back[...] = dot_t(rounded[...], matrix[...])

        def join_back(i):
            rows = tile_at(i)
            total = grad[rows].astype(F32) + wide[0, rows].astype(BF).astype(F32) + back[rows]
            grad[rows] = total.astype(BF)

        loop(OWN // TILE, join_back)
        totals[b].core_finish()
        totals[b].a_start()

    trunk_grad[...] = grad[...]
    table_term = dot(one_hot.astype(BF), grad[...])
    small.value[pl.ds(0, 4)] = table_term[0:4, :MID]
    small.value[pl.ds(4, 4)] = table_term[0:4, MID:]
    for b in range(LAYERS):
        term = jnp.sum(gain_acc[b], axis=0, keepdims=True)
        small.value[pl.ds(8 + 2 * b, 1)] = term[:, :MID]
        small.value[pl.ds(9 + 2 * b, 1)] = term[:, MID:]
        small.value[pl.ds(12 + b, 1)] = jnp.sum(mid_acc[b], axis=0, keepdims=True)
    small.value[pl.ds(14, 2)] = jnp.zeros((2, MID), F32)
    small.core_start()
    totals[1].c_finish()
    first = totals[1].gather_start(1)
    small.core_finish()
    small.ring_start(0)
    totals[0].a_finish()
    totals[0].b_start()
    for copy in first:
        copy.wait()
    first = totals[1].gather_start(0)
    small.ring_finish(0)
    small.ring_start(1)
    totals[0].b_finish()
    totals[0].c_start()
    small.ring_finish(1)
    small.ring_start(2)
    totals[0].c_finish()
    second = totals[0].gather_start(1)
    for copy in first:
        copy.wait()
    first = totals[1].last_start()
    small_out[...] = small.ring_finish(2)
    for copy in second:
        copy.wait()
    second = totals[0].gather_start(0)
    first.wait()
    for copy in second:
        copy.wait()
    totals[0].last_start().wait()


def whole_step(trunk, tokens, table, conv_w, out_w, norm_gain, mid_gain, perm, dilation, cotangent):
    vmem = pl.BlockSpec(memory_space=pltpu.VMEM)
    stay = pl.BlockSpec(memory_space=pl.ANY)
    smem = pl.BlockSpec(memory_space=pltpu.SMEM)
    scratch = [
        pltpu.VMEM((LAYERS, 3, CH, MID), BF),
        pltpu.VMEM((LAYERS, MID, CH), BF),
        pltpu.VMEM((CH, CH), BF),
        pltpu.VMEM((LAYERS, 2, OWN, WIDE), BF),
        pltpu.VMEM((LAYERS, WIDE, CH), BF),
        pltpu.VMEM((WIDE, CH), F32),
        pltpu.VMEM((LAYERS, WIDE, 2 * CH), BF),
        pltpu.VMEM((2, OWN, CH), BF),
        pltpu.VMEM((2, OWN, CH), BF),
        pltpu.VMEM((LAYERS, 2, OWN, CH), F32),
        pltpu.VMEM((LAYERS, 2, OWN, CH), F32),
        pltpu.VMEM((LAYERS, OWN, 128), F32),
        pltpu.VMEM((2, OWN, MID), F32),
        pltpu.VMEM((LAYERS, 2, OWN, MID), F32),
        pltpu.VMEM((LAYERS, 2, OWN, MID), F32),
        pltpu.VMEM((LAYERS, 2, OWN, 128), F32),
        pltpu.VMEM((LAYERS, 2, OWN, MID), BF),
        pltpu.VMEM((2, OWN, CH), F32),
        pltpu.VMEM((OWN, CH), F32),
        pltpu.VMEM((OWN, CH), BF),
        pltpu.VMEM((2 * OWN, CH), BF),
        pltpu.VMEM((LAYERS, WIDE, 2 * MID), BF),
        pltpu.VMEM((2, OWN, MID), BF),
        pltpu.VMEM((2, OWN, MID), BF),
        pltpu.VMEM((OWN, CH), BF),
        pltpu.VMEM((LAYERS, 8, CH), F32),
        pltpu.VMEM((LAYERS, 8, MID), F32),
        pltpu.SemaphoreType.DMA((2,)),
        pltpu.SemaphoreType.DMA((8,)),
        pltpu.SemaphoreType.DMA((8,)),
        pltpu.VMEM((LAYERS, GROWS, LANES), BF),
    ]
    small = [pltpu.VMEM((SMALL, LANES), F32)] + small_scratch()
    return pl.pallas_call(
        step_kernel,
        out_shape=(
            jax.ShapeDtypeStruct((OWN, CH), BF),
            jax.ShapeDtypeStruct((OWN, CH), BF),
            jax.ShapeDtypeStruct((LAYERS, GROWS, LANES), BF),
            jax.ShapeDtypeStruct((SMALL, LANES), F32),
        ),
        in_specs=[smem] + [vmem] * 7 + [stay] * 2,
        out_specs=(vmem,) * 4,
        scratch_shapes=scratch + total_scratch() * 2 + small,
        compiler_params=pltpu.CompilerParams(collective_id=0, has_side_effects=True, vmem_limit_bytes=56 * 1024 * 1024),
        cost_estimate=pl.CostEstimate(flops=10**10, bytes_accessed=2 * 10**7, transcendentals=0),
        name="step",
    )(dilation, trunk, tokens, table, norm_gain, mid_gain, perm, cotangent, conv_w, out_w)


def unpack_grads(result):
    result = result.astype(F32)
    conv = result[:, :2304].reshape(LAYERS, 3, CH, MID)
    out = jnp.concatenate([result[:, 2304:2688], result[:, 2688:]], axis=2)
    return conv, out


def shards(trunk_input, tokens, token_table, conv_weight, out_weight, norm_gain, mid_gain, strand_perm, dilation, out_cotangent):
    table = jnp.pad(token_table, ((0, 4), (0, 0)))
    block_out, trunk_grad, result, small = whole_step(
        trunk_input[0], tokens, table, conv_weight, out_weight, norm_gain, mid_gain, strand_perm[None], dilation, out_cotangent[0])
    conv_total, out_total = unpack_grads(result)
    table_total = jnp.concatenate([small[:4], small[4:8]], axis=1)
    gain_total = small[8:12].reshape(LAYERS, CH)
    return (block_out[None], trunk_grad[None], table_total, conv_total, out_total, gain_total, small[12:14])


def solution(mesh):
    placed = (P("dp", "ctx", None), P("dp", "ctx"), P(), P(), P(), P(), P(), P(), P(), P("dp", "ctx", None))
    return jax.shard_map(
        shards,
        mesh=mesh,
        in_specs=placed,
        out_specs=(P("dp", "ctx", None), P("dp", "ctx", None), P(), P(), P(), P(), P()),
        check_vma=False,
    )
```

profile of v0, /device:TPU:1, one launch (start us, length us, event | category | flops | bytes accessed | tf_op | source)
XLA Modules:
  0.0 109.3 jit_solution(14231044056854523009)
XLA Ops:
  0.6 1.3 %broadcast_in_dim.9.perm = s32[1,768]{1,0:T(1,128)} reshape(s32[768]{0:T(1024)} %param.17) | data formatting | bytes 6144 | tf_op jit(solution)/shard_map/broadcast_in_dim | solution.py:588
  1.9 1.3 %pad.4.table = f32[8,768]{1,0:T(8,128)} pad(f32[4,768]{1,0:T(4,128)} %param.12, f32[]{:T(128)} %constant.2.clone.1), padding=0_4x0_0 | pad | bytes 36868 | tf_op jit(solution)/shard_map/jit(_pad)/pad | solution.py:586
  3.2 94.7 %step.1 = (bf16[256,768]{1,0:T(8,128)(2,1)}, bf16[256,768]{1,0:T(8,128)(2,1)}, bf16[2,3072,384]{2,1,0:T(8,128)(2,1)}, f32[16,384]{1,0:T(8,128)}) custom-call(s32[2]{0:T(128)} %dilation.1, bf16[256,768]{1,0:T(8,128)(2,1)} %bitcast.10, s32[1,256]{1,0:T(1,128)} %tokens.1, f32[8,768]{1,0:T(8,128)} %pad.4.table, f32[2,768]{1,0:T(2,128)} %norm_gain.1, ...), custom_call_target="tpu_custom_call" | custom-call | flops 10000000000 | bytes 20000000 | tf_op jit(solution)/shard_map/step/pallas_call | solution.py:561
  97.9 0.0 slice-start
  97.9 1.3 %slice.27 = f32[2,384]{1,0:T(2,128)} slice(f32[16,384]{1,0:T(8,128)} %get-tuple-element.13), slice={[12:14], [0:384]} | slice | bytes 6144 | tf_op jit(solution)/shard_map/slice | solution.py:592
  99.2 0.8 fusion.1
  100.0 0.6 reshape.21
  100.6 0.6 pad_maximum_fusion.1
  101.2 0.0 slice-start.1
  101.2 1.5 %fusion = (f32[2,384,384]{2,1,0:T(8,128)S(1)}, f32[2,384,384]{2,1,0:T(8,128)S(1)}) fusion(bf16[2,3072,384]{2,1,0:T(8,128)(2,1)} %get-tuple-element.14), kind=kLoop, calls=%fused_computation.2 | loop fusion | bytes 4718592 | tf_op jit(solution)/shard_map/slice | solution.py:581
  102.8 1.6 %pad_maximum_fusion = f32[2,384,768]{2,1,0:T(8,128)} fusion(f32[2,384,384]{2,1,0:T(8,128)S(1)} %get-tuple-element.16, f32[2,384,384]{2,1,0:T(8,128)S(1)} %get-tuple-element.15), kind=kLoop, calls=%fused_computation | loop fusion | flops 589824 | bytes 4718592 | tf_op jit(solution)/shard_map/concatenate | solution.py:581
  104.4 0.0 slice-done
  104.4 0.0 slice-done.1
  104.4 0.0 copy-start.1
  104.4 0.0 copy-start
  104.4 3.4 %slice.28 = f32[2,2304,384]{2,1,0:T(8,128)} slice(bf16[2,3072,384]{2,1,0:T(8,128)(2,1)S(1)} %bitcast.6), slice={[0:2], [0:2304], [0:384]} | slice | bytes 14155776 | tf_op jit(solution)/shard_map/slice | solution.py:580
  107.8 0.0 copy-done.1
  107.8 0.7 copy.19
  108.6 0.0 copy-done
  108.6 0.7 copy.20
  (1 shorter events, 0.0 us)
Async XLA Ops:
  97.9 6.5 %slice-start = ((s8[4718592]{0:T(1024)(128)(4,1)}), s8[524288]{0:T(1024)(128)(4,1)S(1)}, s32[]{:S(2)}) async-start(s8[4718592]{0:T(1024)(128)(4,1)} %bitcast.5), calls=%async_computation | async-start | bytes 1048576
  101.2 3.1 %slice-start.1 = ((s8[4718592]{0:T(1024)(128)(4,1)}), s8[4194304]{0:T(1024)(128)(4,1)S(1)}, s32[]{:S(2)}) async-start(s8[4718592]{0:T(1024)(128)(4,1)} %bitcast.5), calls=%async_computation.1 | async-start | bytes 8388608
  104.4 3.4 %copy-start.1 = (bf16[256,768]{1,0:T(8,128)(2,1)S(1)}, bf16[256,768]{1,0:T(8,128)(2,1)}, u32[]{:S(2)}) copy-start(bf16[256,768]{1,0:T(8,128)(2,1)} %get-tuple-element.11) | copy-start | bytes 1179652
  104.4 4.2 %copy-start = (bf16[256,768]{1,0:T(8,128)(2,1)S(1)}, bf16[256,768]{1,0:T(8,128)(2,1)}, u32[]{:S(2)}) copy-start(bf16[256,768]{1,0:T(8,128)(2,1)} %get-tuple-element.12) | copy-start | bytes 1179652
where the time goes:
time: 110 us; the launch traced here: 109 us
  Pallas kernels  94.7 us (86%)
  local copies, waits for them, and re-layouts  11.8 us (11%)
  other arithmetic  2.19 us (2%)
    pallas_call x1, Pallas kernels, whole_step(): pl.pallas_call(step_kernel, out_shape=(jax.ShapeDtypeStruct((OWN, CH), BF...  94.7 us
    slice x1, local copies, waits for them, and re-layouts, unpack_grads(): conv = result[:, :2304].reshape(LAYERS, 3, CH, MID)  3.42 us

commit v1 on v0

--- a/solution.py
+++ b/solution.py
@@ -269,8 +269,14 @@
 
 
 def gelu_pair(z):
-    below = 0.5 + 0.5 * lax.erf(z * 0.7071067811865476)
-    return z * below, below + z * (0.3989422804014327 * jnp.exp(-0.5 * z * z))
+    size = 1.0 + 0.23164189 * jnp.abs(z)
+    t = pl.reciprocal(size, approx=True)
+    t = t * (2.0 - size * t)
+    bell = jnp.exp(-0.5 * z * z)
+    tail = t * (0.127414796 + t * (-0.142248368 + t * (0.7107068705 + t * (-0.7265760135 + t * 0.5307027145))))
+    tail = tail * bell
+    below = jnp.where(z >= 0.0, 1.0 - tail, tail)
+    return z * below, below + z * (0.3989422804014327 * bell)
 
 
 def norm_back(dz, hat, scale, gain):
@@ -286,7 +292,8 @@
 
 def step_kernel(
     dilation, trunk, tokens, table, norm_gain, mid_gain, perm, cotangent, conv_hbm, out_hbm,
-    block_out, trunk_grad, result, small_out,
+    block_hbm, trunk_hbm, conv_grads, out_grads, table_grad, gain_grad, mid_grad,
+    block_out, table_pad, result, result_sem,
     conv_w, out_w, matrix, move, hidden, relabelled, u_pad, u_low, u_high, hat, slope, scale, mid,
     mid_hat, mid_slope, mid_scale, q, wide, back, rounded, e, dm_pad, dm_low, dm_high, grad, gain_acc, mid_acc,
     weight_sem, halo_send, halo_recv, grads, *scratch,
@@ -315,8 +322,22 @@
             halos.start(2 * index + 1, mine.at[pl.ds(OWN, DMAX)], mine.at[pl.ds(0, DMAX)], right),
         ]
 
+    leaving = []
+
+    def leave(source, target):
+        copy = pltpu.make_async_copy(source, target, result_sem.at[len(leaving)])
+        copy.start()
+        leaving.append(copy)
+
+    def leave_sums(b):
+        leave(result.at[b, pl.ds(0, 2304)], conv_grads.at[b])
+        for s in range(2):
+            leave(result.at[b, pl.ds(2304 + s * MID, MID)], out_grads.at[b, :, strand(s, MID)])
+
+    table_pad[...] = jnp.zeros_like(table_pad)
+    table_pad[pl.ds(0, 4)] = table[...]
     one_hot = (tokens[...] == lax.broadcasted_iota(jnp.int32, (8, OWN), 0)).astype(F32)
-    added = lax.dot_general(one_hot, table[...], (((0,), (0,)), ((), ())), precision=lax.Precision.HIGHEST, preferred_element_type=F32)
+    added = lax.dot_general(one_hot, table_pad[...], (((0,), (0,)), ((), ())), precision=lax.Precision.HIGHEST, preferred_element_type=F32)
     hidden[0, pl.ds(DMAX, OWN)] = (trunk[...].astype(F32) + added).astype(BF)
     greet(spot, (left, right))
     pending = trade(0, hidden.at[0])
@@ -324,7 +345,7 @@
     def fill_matrix(index):
         rows = tile_at(index)
         channel = lax.broadcasted_iota(jnp.int32, (TILE, CH), 0) + index * TILE
-        matrix[rows] = jnp.where(channel == perm[...], 1.0, 0.0).astype(BF)
+        matrix[rows] = jnp.where(channel == perm[...][None, :], 1.0, 0.0).astype(BF)
 
     loop(CH // TILE, fill_matrix)
     bin_from = lax.broadcasted_iota(jnp.int32, (OWN, WIDE), 1)
@@ -400,6 +421,7 @@
         if b + 1 < LAYERS:
             pending = trade(b + 1, hidden.at[b + 1])
 
+    leave(block_out, block_hbm)
     grad[...] = cotangent[...]
     gain_acc[...] = jnp.zeros_like(gain_acc)
     mid_acc[...] = jnp.zeros_like(mid_acc)
@@ -479,7 +501,7 @@
         totals[b].core_finish()
         totals[b].a_start()
 
-    trunk_grad[...] = grad[...]
+    leave(grad, trunk_hbm)
     table_term = dot(one_hot.astype(BF), grad[...])
     small.value[pl.ds(0, 4)] = table_term[0:4, :MID]
     small.value[pl.ds(4, 4)] = table_term[0:4, MID:]
@@ -510,14 +532,24 @@
     for copy in first:
         copy.wait()
     first = totals[1].last_start()
-    small_out[...] = small.ring_finish(2)
+    sums = small.ring_finish(2)
+    table_grad[:, pl.ds(0, MID)] = sums[0:4]
+    table_grad[:, pl.ds(MID, MID)] = sums[4:8]
+    for b in range(LAYERS):
+        gain_grad[pl.ds(b, 1), pl.ds(0, MID)] = sums[8 + 2 * b:9 + 2 * b]
+        gain_grad[pl.ds(b, 1), pl.ds(MID, MID)] = sums[9 + 2 * b:10 + 2 * b]
+    mid_grad[...] = sums[12:14]
     for copy in second:
         copy.wait()
     second = totals[0].gather_start(0)
     first.wait()
+    leave_sums(1)
     for copy in second:
         copy.wait()
     totals[0].last_start().wait()
+    leave_sums(0)
+    for copy in leaving:
+        copy.wait()
 
 
 def whole_step(trunk, tokens, table, conv_w, out_w, norm_gain, mid_gain, perm, dilation, cotangent):
@@ -525,6 +557,10 @@
     stay = pl.BlockSpec(memory_space=pl.ANY)
     smem = pl.BlockSpec(memory_space=pltpu.SMEM)
     scratch = [
+        pltpu.VMEM((OWN, CH), BF),
+        pltpu.VMEM((8, CH), F32),
+        pltpu.VMEM((LAYERS, GROWS, LANES), BF),
+        pltpu.SemaphoreType.DMA((8,)),
         pltpu.VMEM((LAYERS, 3, CH, MID), BF),
         pltpu.VMEM((LAYERS, MID, CH), BF),
         pltpu.VMEM((CH, CH), BF),
@@ -563,11 +599,14 @@
         out_shape=(
             jax.ShapeDtypeStruct((OWN, CH), BF),
             jax.ShapeDtypeStruct((OWN, CH), BF),
-            jax.ShapeDtypeStruct((LAYERS, GROWS, LANES), BF),
-            jax.ShapeDtypeStruct((SMALL, LANES), F32),
+            jax.ShapeDtypeStruct((LAYERS, 3 * CH, MID), BF),
+            jax.ShapeDtypeStruct((LAYERS, MID, CH), BF),
+            jax.ShapeDtypeStruct((4, CH), F32),
+            jax.ShapeDtypeStruct((LAYERS, CH), F32),
+            jax.ShapeDtypeStruct((LAYERS, MID), F32),
         ),
         in_specs=[smem] + [vmem] * 7 + [stay] * 2,
-        out_specs=(vmem,) * 4,
+        out_specs=(stay,) * 4 + (vmem,) * 3,
         scratch_shapes=scratch + total_scratch() * 2 + small,
         compiler_params=pltpu.CompilerParams(collective_id=0, has_side_effects=True, vmem_limit_bytes=56 * 1024 * 1024),
         cost_estimate=pl.CostEstimate(flops=10**10, bytes_accessed=2 * 10**7, transcendentals=0),
@@ -575,21 +614,11 @@
     )(dilation, trunk, tokens, table, norm_gain, mid_gain, perm, cotangent, conv_w, out_w)
 
 
-def unpack_grads(result):
-    result = result.astype(F32)
-    conv = result[:, :2304].reshape(LAYERS, 3, CH, MID)
-    out = jnp.concatenate([result[:, 2304:2688], result[:, 2688:]], axis=2)
-    return conv, out
-
-
 def shards(trunk_input, tokens, token_table, conv_weight, out_weight, norm_gain, mid_gain, strand_perm, dilation, out_cotangent):
-    table = jnp.pad(token_table, ((0, 4), (0, 0)))
-    block_out, trunk_grad, result, small = whole_step(
-        trunk_input[0], tokens, table, conv_weight, out_weight, norm_gain, mid_gain, strand_perm[None], dilation, out_cotangent[0])
-    conv_total, out_total = unpack_grads(result)
-    table_total = jnp.concatenate([small[:4], small[4:8]], axis=1)
-    gain_total = small[8:12].reshape(LAYERS, CH)
-    return (block_out[None], trunk_grad[None], table_total, conv_total, out_total, gain_total, small[12:14])
+    block_out, trunk_grad, conv_total, out_total, table_total, gain_total, mid_total = whole_step(
+        trunk_input[0], tokens, token_table, conv_weight, out_weight, norm_gain, mid_gain, strand_perm, dilation, out_cotangent[0])
+    conv_total = conv_total.astype(F32).reshape(LAYERS, 3, CH, MID)
+    return (block_out[None], trunk_grad[None], table_total, conv_total, out_total.astype(F32), gain_total, mid_total)
 
 
 def solution(mesh):

time: 110 us -> 108 us (0.982)
  local copies, waits for them, and re-layouts: 11.8 us -> 3.29 us
  other arithmetic: 2.19 us -> 7.13 us
  Pallas kernels: 94.7 us -> 96.9 us
    slice x4 -> x0, local copies, waits for them, and re-layouts: 7.1 us -> none  [the longest x1 3.42 us: unpack_grads(): conv = result[:, :2304].reshape(LAYERS, 3, CH, MID)]
    reshape x0 -> x1, other arithmetic: none -> 5.55 us  [shards(): conv_total = conv_total.astype(F32).reshape(LAYERS, 3, CH, MID)]
    pallas_call x1, Pallas kernels: 94.7 us -> 96.9 us  [whole_step(): pl.pallas_call(step_kernel, out_shape=(jax.ShapeDtypeStruct((OWN, CH), BF...]
    concatenate x2 -> x0, other arithmetic: 2.19 us -> none  [the longest x1 1.59 us: unpack_grads(): out = jnp.concatenate([result[:, 2304:2688], result[:, 2688:]], axis=2)]
    unnamed x10 -> x17, local copies, waits for them, and re-layouts: 1.51 us -> 3.29 us
    convert_element_type x0 -> x1, other arithmetic: none -> 1.58 us  [shards(): out_total.astype(F32)]
    pad x1 -> x0, local copies, waits for them, and re-layouts: 1.32 us -> none  [shards(): table = jnp.pad(token_table, ((0, 4), (0, 0)))]
    broadcast_in_dim x1 -> x0, local copies, waits for them, and re-layouts: 1.27 us -> none  [shards(): strand_perm[None]]
where the time goes in v1:
time: 108 us
  Pallas kernels  96.9 us (90%)
  other arithmetic  7.13 us (7%)
  local copies, waits for them, and re-layouts  3.29 us (3%)
    pallas_call x1, Pallas kernels, whole_step(): pl.pallas_call(step_kernel, out_shape=(jax.ShapeDtypeStruct((OWN, CH), BF...  96.9 us
    reshape x1, other arithmetic, shards(): conv_total = conv_total.astype(F32).reshape(LAYERS, 3, CH, MID)  5.55 us
    unnamed x17, local copies, waits for them, and re-layouts  3.29 us

profile of v1, /device:TPU:1, one launch (start us, length us, event | category | flops | bytes accessed | tf_op | source)
XLA Modules:
  0.0 108.0 jit_solution(15569294939641443267)
XLA Ops:
  0.6 96.9 %step.1 = (bf16[256,768]{1,0:T(8,128)(2,1)}, bf16[256,768]{1,0:T(8,128)(2,1)}, bf16[2,2304,384]{2,1,0:T(8,128)(2,1)}, bf16[2,384,768]{2,1,0:T(8,128)(2,1)}, f32[...) custom-call(s32[2]{0:T(128)} %dilation.1, bf16[256,768]{1,0:T(8,128)(2,1)} %bitcast.9, s32[1,256]{1,0:T(1,128)} %tokens.1, ...), custom_call_target="tpu_custom_call" | custom-call | flops 10000000000 | bytes 20000000 | tf_op jit(solution)/shard_map/step/pallas_call | solution.py:597
  97.6 0.0 copy-start
  97.6 5.5 %convert.1 = f32[2,3,768,384]{3,2,1,0:T(8,128)} convert(bf16[2,3,768,384]{3,2,1,0:T(8,128)(2,1)} %bitcast.6) | non-fusion elementwise | flops 1769472 | bytes 10616832 | tf_op jit(solution)/shard_map/reshape | solution.py:620
  103.1 0.0 copy-start.2
  103.1 0.0 copy-start.1
  103.1 0.0 copy-start.3
  103.1 0.0 copy-start.4
  103.1 0.0 copy-start.5
  103.1 0.0 copy-done
  103.2 1.6 %convert_element_type.4 = f32[2,384,768]{2,1,0:T(8,128)} convert(bf16[2,384,768]{2,1,0:T(8,128)(2,1)S(1)} %copy-done) | non-fusion elementwise | flops 589824 | bytes 3538944 | tf_op jit(solution)/shard_map/convert_element_type | solution.py:621
  104.7 0.0 copy-done.2
  104.7 0.7 copy.22
  105.5 0.0 copy-done.1
  105.5 0.7 copy.23
  106.2 0.0 copy-done.3
  106.2 0.6 copy.24
  106.8 0.0 copy-done.4
  106.8 0.6 copy.25
  107.4 0.0 copy-done.5
  107.4 0.6 copy.26
Async XLA Ops:
  97.6 5.6 %copy-start = (bf16[2,384,768]{2,1,0:T(8,128)(2,1)S(1)}, bf16[2,384,768]{2,1,0:T(8,128)(2,1)}, u32[]{:S(2)}) copy-start(bf16[2,384,768]{2,1,0:T(8,128)(2,1)} %get-tuple-element.18) | copy-start | bytes 3538948
  103.1 1.6 %copy-start.2 = (bf16[256,768]{1,0:T(8,128)(2,1)S(1)}, bf16[256,768]{1,0:T(8,128)(2,1)}, u32[]{:S(2)}) copy-start(bf16[256,768]{1,0:T(8,128)(2,1)} %get-tuple-element.14) | copy-start | bytes 1179652
  103.1 2.4 %copy-start.1 = (bf16[256,768]{1,0:T(8,128)(2,1)S(1)}, bf16[256,768]{1,0:T(8,128)(2,1)}, u32[]{:S(2)}) copy-start(bf16[256,768]{1,0:T(8,128)(2,1)} %get-tuple-element.15) | copy-start | bytes 1179652
  103.1 3.1 %copy-start.3 = (f32[4,768]{1,0:T(4,128)S(1)}, f32[4,768]{1,0:T(4,128)}, u32[]{:S(2)}) copy-start(f32[4,768]{1,0:T(4,128)} %get-tuple-element.30) | copy-start | bytes 36868
  103.1 3.7 %copy-start.4 = (f32[2,768]{1,0:T(2,128)S(1)}, f32[2,768]{1,0:T(2,128)}, u32[]{:S(2)}) copy-start(f32[2,768]{1,0:T(2,128)} %get-tuple-element.33) | copy-start | bytes 18436
  103.1 4.3 %copy-start.5 = (f32[2,384]{1,0:T(2,128)S(1)}, f32[2,384]{1,0:T(2,128)}, u32[]{:S(2)}) copy-start(f32[2,384]{1,0:T(2,128)} %get-tuple-element.34) | copy-start | bytes 9220

commit v2 on v1

--- a/solution.py
+++ b/solution.py
@@ -143,23 +143,45 @@
             _, eighth = self.rows_of(third)
             self.result[pl.ds(pl.multiple_of(eighth, 32), EIGHTH), self.lanes(third)] = total.astype(jnp.bfloat16)
 
-    def gather_start(self, which):
+    def gather(self, which):
         copies = []
         for third, order in enumerate(ORDERS):
             quarter, eighth = self.rows_of(third)
             rows = pl.ds(eighth, EIGHTH) if which else pl.ds(quarter, QUARTER)
             piece = self.result.at[rows, self.lanes(third)]
-            for distance in (2, 1, 3):
+            for distance in (1, 3, 2):
                 copies.append(self.copies.start(
                     28 + which * 9 + third * 3 + distance - 1, piece, piece, ring_peer(self.spot, order[which], distance)))
         return copies
 
-    def last_start(self):
-        piece = self.result.at[pl.ds(self.base, HALF)]
-        return self.copies.start(46, piece, piece, core_peer(self.spot))
-
-
-TOTAL_COPIES = 47
+    def b_gather(self):
+        self.late = self.gather(1)
+
+    def pass_on(self, third, distance):
+        quarter = lax.rem(self.spot[ORDERS[third][0]] + 4 - distance, 4)
+        piece = self.result.at[pl.ds(self.base + quarter * QUARTER, QUARTER), self.lanes(third)]
+        self.last.append(self.copies.start(46 + third * 4 + distance, piece, piece, core_peer(self.spot)))
+
+    def a_gather(self):
+        for copy in self.late:
+            copy.wait()
+        self.late = self.gather(0)
+        self.last = []
+        for third in range(3):
+            self.pass_on(third, 0)
+
+    def forward(self):
+        for slot, distance in enumerate((1, 3, 2)):
+            for third in range(3):
+                self.late[third * 3 + slot].wait()
+                self.pass_on(third, distance)
+
+    def finish(self):
+        for copy in self.last:
+            copy.wait()
+
+
+TOTAL_COPIES = 58
 
 
 def total_scratch():
@@ -228,7 +250,7 @@
 WIDE = OWN + 2 * DMAX
 CH = 768
 MID = 384
-TILE = 32
+TILE = 64
 BF = jnp.bfloat16
 F32 = jnp.float32
 
@@ -254,7 +276,7 @@
         body(index)
         return carry
 
-    lax.fori_loop(0, count, step, 0)
+    lax.fori_loop(0, count, step, 0, unroll=2 if count % 2 == 0 else 1)
 
 
 def tile_at(index, base=0, size=TILE):
@@ -388,10 +410,10 @@
             loop(DMAX // TILE, lambda i: front(tile_at(i, base), None))
 
         for s in range(2):
-            u_low[s] = dot(move[b, s], u_pad[b, :, strand(s)]).astype(BF)
-            u_high[s] = dot(move[b, 1 - s], u_pad[b, :, strand(s)]).astype(BF)
-        for s in range(2):
-            mid[s] += dot(u_low[s], conv_w[b, 0]) + dot(u_high[s], conv_w[b, 2])
+            u_low[b, s] = dot(move[b, s], u_pad[b, :, strand(s)]).astype(BF)
+            u_high[b, s] = dot(move[b, 1 - s], u_pad[b, :, strand(s)]).astype(BF)
+        for s in range(2):
+            mid[s] += dot(u_low[b, s], conv_w[b, 0]) + dot(u_high[b, s], conv_w[b, 2])
 
         def middle(i):
             rows = tile_at(i)
@@ -448,9 +470,6 @@
 
         loop(OWN // TILE, middle_back)
         pending = trade(LAYERS + b, dm_pad.at[b])
-        if b == 0:
-            totals[1].a_finish()
-            totals[1].b_start()
         q_all = q[b].reshape(2 * OWN, MID)
         out_grad = dot_rows(q_all, e[...])
         sums[pl.ds(2304, MID)] = out_grad[:, :MID].astype(BF)
@@ -458,22 +477,26 @@
         own = pl.ds(DMAX, OWN)
         u_all = jnp.concatenate([u_pad[b, own, strand(s)] for s in range(2)], axis=0)
         dm_all = jnp.concatenate([dm_pad[b, own, strand(s, MID)] for s in range(2)], axis=0)
-        sums[pl.ds(CH, CH)] = dot_rows(u_all, dm_all).astype(BF)
+        for tap, left_side in enumerate((u_low[b].reshape(2 * OWN, CH), u_all, u_high[b].reshape(2 * OWN, CH))):
+            sums[pl.ds(tap * CH, CH)] = dot_rows(left_side, dm_all).astype(BF)
+        totals[b].core_start()
         for s in range(2):
             wide[s] = dot_t(dm_pad[b, own, strand(s, MID)], conv_w[b, 1])
+        if b == 0:
+            totals[1].a_finish()
+            totals[1].b_start()
         for copy in pending:
             copy.wait()
         for s in range(2):
             dm_low[s] = dot(move[b, 1 - s], dm_pad[b, :, strand(s, MID)]).astype(BF)
             dm_high[s] = dot(move[b, s], dm_pad[b, :, strand(s, MID)]).astype(BF)
-        sums[pl.ds(0, CH)] = dot_rows(u_all, dm_low[...].reshape(2 * OWN, MID)).astype(BF)
-        sums[pl.ds(2 * CH, CH)] = dot_rows(u_all, dm_high[...].reshape(2 * OWN, MID)).astype(BF)
-        totals[b].core_start()
+        for s in range(2):
+            wide[s] += dot_t(dm_low[s], conv_w[b, 0]) + dot_t(dm_high[s], conv_w[b, 2])
+        totals[b].core_finish()
+        totals[b].a_start()
         if b == 0:
             totals[1].b_finish()
             totals[1].c_start()
-        for s in range(2):
-            wide[s] += dot_t(dm_low[s], conv_w[b, 0]) + dot_t(dm_high[s], conv_w[b, 2])
 
         def front_back(i):
             rows = tile_at(i)
@@ -498,8 +521,6 @@
             grad[rows] = total.astype(BF)
 
         loop(OWN // TILE, join_back)
-        totals[b].core_finish()
-        totals[b].a_start()
 
     leave(grad, trunk_hbm)
     table_term = dot(one_hot.astype(BF), grad[...])
@@ -513,25 +534,24 @@
     small.value[pl.ds(14, 2)] = jnp.zeros((2, MID), F32)
     small.core_start()
     totals[1].c_finish()
-    first = totals[1].gather_start(1)
+    totals[1].b_gather()
+    totals[0].a_finish()
+    totals[0].b_start()
     small.core_finish()
     small.ring_start(0)
-    totals[0].a_finish()
-    totals[0].b_start()
-    for copy in first:
-        copy.wait()
-    first = totals[1].gather_start(0)
+    totals[1].a_gather()
+    totals[0].b_finish()
+    totals[0].c_start()
     small.ring_finish(0)
     small.ring_start(1)
-    totals[0].b_finish()
-    totals[0].c_start()
+    totals[0].c_finish()
+    totals[0].b_gather()
+    totals[1].forward()
     small.ring_finish(1)
     small.ring_start(2)
-    totals[0].c_finish()
-    second = totals[0].gather_start(1)
-    for copy in first:
-        copy.wait()
-    first = totals[1].last_start()
+    totals[0].a_gather()
+    totals[1].finish()
+    leave_sums(1)
     sums = small.ring_finish(2)
     table_grad[:, pl.ds(0, MID)] = sums[0:4]
     table_grad[:, pl.ds(MID, MID)] = sums[4:8]
@@ -539,14 +559,8 @@
         gain_grad[pl.ds(b, 1), pl.ds(0, MID)] = sums[8 + 2 * b:9 + 2 * b]
         gain_grad[pl.ds(b, 1), pl.ds(MID, MID)] = sums[9 + 2 * b:10 + 2 * b]
     mid_grad[...] = sums[12:14]
-    for copy in second:
-        copy.wait()
-    second = totals[0].gather_start(0)
-    first.wait()
-    leave_sums(1)
-    for copy in second:
-        copy.wait()
-    totals[0].last_start().wait()
+    totals[0].forward()
+    totals[0].finish()
     leave_sums(0)
     for copy in leaving:
         copy.wait()
@@ -568,8 +582,8 @@
         pltpu.VMEM((LAYERS, WIDE, CH), BF),
         pltpu.VMEM((WIDE, CH), F32),
         pltpu.VMEM((LAYERS, WIDE, 2 * CH), BF),
-        pltpu.VMEM((2, OWN, CH), BF),
-        pltpu.VMEM((2, OWN, CH), BF),
+        pltpu.VMEM((LAYERS, 2, OWN, CH), BF),
+        pltpu.VMEM((LAYERS, 2, OWN, CH), BF),
         pltpu.VMEM((LAYERS, 2, OWN, CH), F32),
         pltpu.VMEM((LAYERS, 2, OWN, CH), F32),
         pltpu.VMEM((LAYERS, OWN, 128), F32),
@@ -614,11 +628,45 @@
     )(dilation, trunk, tokens, table, norm_gain, mid_gain, perm, cotangent, conv_w, out_w)
 
 
+def widen_kernel(conv_in, out_in, block_in, trunk_in, table_in, gain_in, mid_in,
+                 conv_out, out_out, block_out, trunk_out, table_out, gain_out, mid_out):
+    conv_out[...] = conv_in[...].astype(F32)
+    out_out[...] = out_in[...].astype(F32)
+    block_out[...] = block_in[...]
+    trunk_out[...] = trunk_in[...]
+    table_out[...] = table_in[...]
+    gain_out[...] = gain_in[...]
+    mid_out[...] = mid_in[...]
+
+
+def widen(*arrays):
+    steps = 4
+
+    def piece(array):
+        if array.shape[0] % (steps * 16) == 0:
+            return pl.BlockSpec((array.shape[0] // steps, array.shape[1]), lambda i: (i, 0))
+        return pl.BlockSpec(array.shape, lambda i: (0, 0))
+
+    specs = [piece(array) for array in arrays]
+    return pl.pallas_call(
+        widen_kernel,
+        grid=(steps,),
+        out_shape=[jax.ShapeDtypeStruct(array.shape, F32 if i < 2 else array.dtype) for i, array in enumerate(arrays)],
+        in_specs=specs,
+        out_specs=specs,
+        compiler_params=pltpu.CompilerParams(vmem_limit_bytes=60 * 1024 * 1024),
+        cost_estimate=pl.CostEstimate(flops=10**6, bytes_accessed=15 * 10**6, transcendentals=0),
+        name="widen",
+    )(*arrays)
+
+
 def shards(trunk_input, tokens, token_table, conv_weight, out_weight, norm_gain, mid_gain, strand_perm, dilation, out_cotangent):
     block_out, trunk_grad, conv_total, out_total, table_total, gain_total, mid_total = whole_step(
         trunk_input[0], tokens, token_table, conv_weight, out_weight, norm_gain, mid_gain, strand_perm, dilation, out_cotangent[0])
-    conv_total = conv_total.astype(F32).reshape(LAYERS, 3, CH, MID)
-    return (block_out[None], trunk_grad[None], table_total, conv_total, out_total.astype(F32), gain_total, mid_total)
+    conv_total, out_total, block_out, trunk_grad, table_total, gain_total, mid_total = widen(
+        conv_total.reshape(LAYERS * 3 * CH, MID), out_total.reshape(LAYERS * MID, CH), block_out, trunk_grad, table_total, gain_total, mid_total)
+    return (block_out[None], trunk_grad[None], table_total, conv_total.reshape(LAYERS, 3, CH, MID),
+            out_total.reshape(LAYERS, MID, CH), gain_total, mid_total)
 
 
 def solution(mesh):

time: 108 us -> 96.8 us (0.90)
  other arithmetic: 7.13 us -> 0 us
  local copies, waits for them, and re-layouts: 3.29 us -> 0 us
  Pallas kernels: 96.9 us -> 95.7 us
    pallas_call x1, Pallas kernels: 96.9 us -> 88.8 us  [whole_step(): pl.pallas_call(step_kernel, out_shape=(jax.ShapeDtypeStruct((OWN, CH), BF...]
    pallas_call x0 -> x1, Pallas kernels: none -> 6.94 us  [widen(): pl.pallas_call(widen_kernel, grid=(steps,), out_shape=[jax.ShapeDtypeStru...]
    reshape x1 -> x0, other arithmetic: 5.55 us -> none  [shards(): conv_total = conv_total.astype(F32).reshape(LAYERS, 3, CH, MID)]
    unnamed x17 -> x0, local copies, waits for them, and re-layouts: 3.29 us -> none
    convert_element_type x1 -> x0, other arithmetic: 1.58 us -> none  [shards(): out_total.astype(F32)]
where the time goes in v2:
time: 96.8 us; the launch traced here: 96.5 us
  Pallas kernels  95.7 us (99%)
    pallas_call x1, Pallas kernels, whole_step(): pl.pallas_call(step_kernel, out_shape=(jax.ShapeDtypeStruct((OWN, CH), BF...  88.8 us
    pallas_call x1, Pallas kernels, widen(): pl.pallas_call(widen_kernel, grid=(steps,), out_shape=[jax.ShapeDtypeStru...  6.94 us

profile of v2, /device:TPU:1, one launch (start us, length us, event | category | flops | bytes accessed | tf_op | source)
XLA Modules:
  0.0 96.5 jit_solution(17314606130654693245)
XLA Ops:
  0.6 88.8 %step.1 = (bf16[256,768]{1,0:T(8,128)(2,1)}, bf16[256,768]{1,0:T(8,128)(2,1)}, bf16[2,2304,384]{2,1,0:T(8,128)(2,1)}, bf16[2,384,768]{2,1,0:T(8,128)(2,1)}, f32[...) custom-call(s32[2]{0:T(128)} %dilation.1, bf16[256,768]{1,0:T(8,128)(2,1)} %bitcast.12, s32[1,256]{1,0:T(1,128)} %tokens.1, ...), custom_call_target="tpu_custom_call" | custom-call | flops 10000000000 | bytes 20000000 | tf_op jit(solution)/shard_map/step/pallas_call | solution.py:611
  89.4 6.9 %widen.1 = (f32[4608,384]{1,0:T(8,128)}, f32[768,768]{1,0:T(8,128)}, bf16[256,768]{1,0:T(8,128)(2,1)}, bf16[256,768]{1,0:T(8,128)(2,1)}, f32[4,768]{1,0:T(4,128)}, /*index=5*/f32[2,768]{1,0:T(2,128)}, f32[2,384]{1,0:T(2,128)}) custom-call(bf16[4608,384]{1,0:T(8,128)(2,1)} %bitcast.8, bf16[768,768]{1,0:T(8,128)(2,1)} %bitcast.9, ...), custom_call_target="tpu_custom_call" | custom-call | flops 1000000 | bytes 15000000 | tf_op jit(solution)/shard_map/widen/pallas_call | solution.py:651

commit v3 on v2

--- a/solution.py
+++ b/solution.py
@@ -89,19 +89,16 @@
                     self.sums0.at[pl.ds(chunk * QUARTER, QUARTER), self.lanes(third)],
                     self.in_a.at[third, distance - 1], ring_peer(self.spot, order[0], distance)))
 
-    def a_finish(self):
-        for copy in self.a:
-            copy.wait()
+    def a_to_b(self):
+        self.b = []
         for third, order in enumerate(ORDERS):
             mine = pl.ds(pl.multiple_of(self.spot[order[0]] * QUARTER, 32), QUARTER)
+            for copy in self.a[third * 3:third * 3 + 3]:
+                copy.wait()
             total = self.sums0[mine, self.lanes(third)].astype(jnp.float32)
             for slot in range(3):
                 total = total + self.in_a[third, slot].astype(jnp.float32)
             self.sums1[third] = total.astype(jnp.bfloat16)
-
-    def b_start(self):
-        self.b = []
-        for third, order in enumerate(ORDERS):
             for distance in (2, 1, 3):
                 chunk = lax.rem(self.spot[order[1]] + distance, 4)
                 self.b.append(self.copies.start(
@@ -109,19 +106,16 @@
                     self.sums1.at[third, pl.ds(chunk * EIGHTH, EIGHTH)],
                     self.in_b.at[third, distance - 1], ring_peer(self.spot, order[1], distance)))
 
-    def b_finish(self):
-        for copy in self.b:
-            copy.wait()
+    def b_to_c(self):
+        self.c = []
         for third, order in enumerate(ORDERS):
             mine = pl.ds(pl.multiple_of(self.spot[order[1]] * EIGHTH, 32), EIGHTH)
+            for copy in self.b[third * 3:third * 3 + 3]:
+                copy.wait()
             total = self.sums1[third, mine].astype(jnp.float32)
             for slot in range(3):
                 total = total + self.in_b[third, slot].astype(jnp.float32)
             self.sums2[third] = total.astype(jnp.bfloat16)
-
-    def c_start(self):
-        self.c = []
-        for third, order in enumerate(ORDERS):
             for distance in (2, 1, 3):
                 self.c.append(self.copies.start(
                     19 + third * 3 + distance - 1, self.sums2.at[third],
@@ -133,29 +127,26 @@
         quarter = self.base + self.spot[order[0]] * QUARTER
         return quarter, quarter + self.spot[order[1]] * EIGHTH
 
-    def c_finish(self):
-        for copy in self.c:
-            copy.wait()
+    def spread(self, third, which):
+        order = ORDERS[third]
+        quarter, eighth = self.rows_of(third)
+        rows = pl.ds(eighth, EIGHTH) if which else pl.ds(quarter, QUARTER)
+        piece = self.result.at[rows, self.lanes(third)]
+        return [
+            self.copies.start(28 + which * 9 + third * 3 + distance - 1, piece, piece, ring_peer(self.spot, order[which], distance))
+            for distance in (1, 3, 2)]
+
+    def c_to_gather(self):
+        self.early = []
         for third in range(3):
+            for copy in self.c[third * 3:third * 3 + 3]:
+                copy.wait()
             total = self.in_c[third, 0].astype(jnp.float32)
             for slot in range(1, 4):
                 total = total + self.in_c[third, slot].astype(jnp.float32)
             _, eighth = self.rows_of(third)
             self.result[pl.ds(pl.multiple_of(eighth, 32), EIGHTH), self.lanes(third)] = total.astype(jnp.bfloat16)
-
-    def gather(self, which):
-        copies = []
-        for third, order in enumerate(ORDERS):
-            quarter, eighth = self.rows_of(third)
-            rows = pl.ds(eighth, EIGHTH) if which else pl.ds(quarter, QUARTER)
-            piece = self.result.at[rows, self.lanes(third)]
-            for distance in (1, 3, 2):
-                copies.append(self.copies.start(
-                    28 + which * 9 + third * 3 + distance - 1, piece, piece, ring_peer(self.spot, order[which], distance)))
-        return copies
-
-    def b_gather(self):
-        self.late = self.gather(1)
+            self.early += self.spread(third, 1)
 
     def pass_on(self, third, distance):
         quarter = lax.rem(self.spot[ORDERS[third][0]] + 4 - distance, 4)
@@ -163,10 +154,11 @@
         self.last.append(self.copies.start(46 + third * 4 + distance, piece, piece, core_peer(self.spot)))
 
     def a_gather(self):
-        for copy in self.late:
-            copy.wait()
-        self.late = self.gather(0)
-        self.last = []
+        self.late, self.last = [], []
+        for third in range(3):
+            for copy in self.early[third * 3:third * 3 + 3]:
+                copy.wait()
+            self.late += self.spread(third, 0)
         for third in range(3):
             self.pass_on(third, 0)
 
@@ -242,7 +234,7 @@
     peers += list(extra)
     for peer in peers:
         pl.semaphore_signal(barrier, inc=1, device_id=peer, device_id_type=MESH)
-    pl.semaphore_wait(barrier, len(peers))
+    return lambda: pl.semaphore_wait(barrier, len(peers))
 
 
 epsilon = 1e-05
@@ -327,6 +319,7 @@
     right = (dp, lax.rem(ctx + 1, 32))
     first_bin = jnp.where(ctx == 0, DMAX, 0)
     end_bin = jnp.where(ctx == 31, DMAX + OWN, WIDE)
+    met = greet(spot, (left, right))
     weights = [
         pltpu.make_async_copy(conv_hbm, conv_w, weight_sem.at[0]),
         pltpu.make_async_copy(out_hbm, out_w, weight_sem.at[1]),
@@ -357,11 +350,16 @@
             leave(result.at[b, pl.ds(2304 + s * MID, MID)], out_grads.at[b, :, strand(s, MID)])
 
     table_pad[...] = jnp.zeros_like(table_pad)
-    table_pad[pl.ds(0, 4)] = table[...]
+    rest = table[...]
+    for part in range(3):
+        piece = rest.astype(BF).astype(F32)
+        table_pad[pl.ds(8 * part, 4)] = piece
+        rest = rest - piece
     one_hot = (tokens[...] == lax.broadcasted_iota(jnp.int32, (8, OWN), 0)).astype(F32)
-    added = lax.dot_general(one_hot, table_pad[...], (((0,), (0,)), ((), ())), precision=lax.Precision.HIGHEST, preferred_element_type=F32)
+    three_hot = jnp.concatenate([one_hot] * 4, axis=0).astype(BF)
+    added = dot_rows(three_hot, table_pad[...].astype(BF))
     hidden[0, pl.ds(DMAX, OWN)] = (trunk[...].astype(F32) + added).astype(BF)
-    greet(spot, (left, right))
+    met()
     pending = trade(0, hidden.at[0])
 
     def fill_matrix(index):
@@ -483,8 +481,7 @@
         for s in range(2):
             wide[s] = dot_t(dm_pad[b, own, strand(s, MID)], conv_w[b, 1])
         if b == 0:
-            totals[1].a_finish()
-            totals[1].b_start()
+            totals[1].a_to_b()
         for copy in pending:
             copy.wait()
         for s in range(2):
@@ -495,8 +492,7 @@
         totals[b].core_finish()
         totals[b].a_start()
         if b == 0:
-            totals[1].b_finish()
-            totals[1].c_start()
+            totals[1].b_to_c()
 
         def front_back(i):
             rows = tile_at(i)
@@ -533,19 +529,15 @@
         small.value[pl.ds(12 + b, 1)] = jnp.sum(mid_acc[b], axis=0, keepdims=True)
     small.value[pl.ds(14, 2)] = jnp.zeros((2, MID), F32)
     small.core_start()
-    totals[1].c_finish()
-    totals[1].b_gather()
-    totals[0].a_finish()
-    totals[0].b_start()
+    totals[1].c_to_gather()
+    totals[0].a_to_b()
     small.core_finish()
     small.ring_start(0)
     totals[1].a_gather()
-    totals[0].b_finish()
-    totals[0].c_start()
+    totals[0].b_to_c()
     small.ring_finish(0)
     small.ring_start(1)
-    totals[0].c_finish()
-    totals[0].b_gather()
+    totals[0].c_to_gather()
     totals[1].forward()
     small.ring_finish(1)
     small.ring_start(2)
@@ -572,7 +564,7 @@
     smem = pl.BlockSpec(memory_space=pltpu.SMEM)
     scratch = [
         pltpu.VMEM((OWN, CH), BF),
-        pltpu.VMEM((8, CH), F32),
+        pltpu.VMEM((32, CH), F32),
         pltpu.VMEM((LAYERS, GROWS, LANES), BF),
         pltpu.SemaphoreType.DMA((8,)),
         pltpu.VMEM((LAYERS, 3, CH, MID), BF),
@@ -628,32 +620,56 @@
     )(dilation, trunk, tokens, table, norm_gain, mid_gain, perm, cotangent, conv_w, out_w)
 
 
+CONV_PIECES = 9
+OUT_PIECES = 3
+
+
 def widen_kernel(conv_in, out_in, block_in, trunk_in, table_in, gain_in, mid_in,
-                 conv_out, out_out, block_out, trunk_out, table_out, gain_out, mid_out):
-    conv_out[...] = conv_in[...].astype(F32)
-    out_out[...] = out_in[...].astype(F32)
-    block_out[...] = block_in[...]
-    trunk_out[...] = trunk_in[...]
-    table_out[...] = table_in[...]
-    gain_out[...] = gain_in[...]
-    mid_out[...] = mid_in[...]
+                 conv_out, out_out, block_out, trunk_out, table_out, gain_out, mid_out,
+                 conv_narrow, out_narrow, conv_wide, out_wide, block_held, trunk_held, table_held, gain_held, mid_held,
+                 in_sem, back_sem):
+    work = []
+    for source, target, narrow, broad, pieces in (
+            (conv_in, conv_out, conv_narrow, conv_wide, CONV_PIECES), (out_in, out_out, out_narrow, out_wide, OUT_PIECES)):
+        size = source.shape[0] // pieces
+        for i in range(pieces):
+            rows = pl.ds(i * size, size)
+            index = len(work)
+            work.append((
+                pltpu.make_async_copy(source.at[rows], narrow.at[rows], in_sem.at[index]),
+                pltpu.make_async_copy(broad.at[rows], target.at[rows], back_sem.at[index]),
+                narrow, broad, rows))
+    for source, target, held in (
+            (block_in, block_out, block_held), (trunk_in, trunk_out, trunk_held), (table_in, table_out, table_held),
+            (gain_in, gain_out, gain_held), (mid_in, mid_out, mid_held)):
+        index = len(work)
+        work.append((
+            pltpu.make_async_copy(source, held, in_sem.at[index]),
+            pltpu.make_async_copy(held, target, back_sem.at[index]), None, None, None))
+    for fetch, *_ in work:
+        fetch.start()
+    for fetch, store, narrow, broad, rows in work:
+        fetch.wait()
+        if narrow is not None:
+            broad[rows] = narrow[rows].astype(F32)
+        store.start()
+    for _, store, *_ in work:
+        store.wait()
 
 
 def widen(*arrays):
-    steps = 4
-
-    def piece(array):
-        if array.shape[0] % (steps * 16) == 0:
-            return pl.BlockSpec((array.shape[0] // steps, array.shape[1]), lambda i: (i, 0))
-        return pl.BlockSpec(array.shape, lambda i: (0, 0))
-
-    specs = [piece(array) for array in arrays]
+    stay = pl.BlockSpec(memory_space=pl.ANY)
+    conv, out = arrays[:2]
     return pl.pallas_call(
         widen_kernel,
-        grid=(steps,),
         out_shape=[jax.ShapeDtypeStruct(array.shape, F32 if i < 2 else array.dtype) for i, array in enumerate(arrays)],
-        in_specs=specs,
-        out_specs=specs,
+        in_specs=[stay] * len(arrays),
+        out_specs=[stay] * len(arrays),
+        scratch_shapes=[
+            pltpu.VMEM(conv.shape, BF), pltpu.VMEM(out.shape, BF), pltpu.VMEM(conv.shape, F32), pltpu.VMEM(out.shape, F32),
+            *[pltpu.VMEM(array.shape, array.dtype) for array in arrays[2:]],
+            pltpu.SemaphoreType.DMA((CONV_PIECES + OUT_PIECES + 5,)), pltpu.SemaphoreType.DMA((CONV_PIECES + OUT_PIECES + 5,)),
+        ],
         compiler_params=pltpu.CompilerParams(vmem_limit_bytes=60 * 1024 * 1024),
         cost_estimate=pl.CostEstimate(flops=10**6, bytes_accessed=15 * 10**6, transcendentals=0),
         name="widen",

time: 96.8 us -> 92.8 us (0.959)
  Pallas kernels: 95.7 us -> 91.8 us
    pallas_call x1, Pallas kernels: 88.8 us -> 86.5 us  [whole_step(): pl.pallas_call(step_kernel, out_shape=(jax.ShapeDtypeStruct((OWN, CH), BF...]
    pallas_call x1, Pallas kernels: 6.94 us -> 5.32 us  [widen(): pl.pallas_call(widen_kernel, out_shape=[jax.ShapeDtypeStruct(array.shape,...]
where the time goes in v3:
time: 92.8 us; the launch traced here: 92.6 us
  Pallas kernels  91.8 us (99%)
    pallas_call x1, Pallas kernels, whole_step(): pl.pallas_call(step_kernel, out_shape=(jax.ShapeDtypeStruct((OWN, CH), BF...  86.5 us
    pallas_call x1, Pallas kernels, widen(): pl.pallas_call(widen_kernel, out_shape=[jax.ShapeDtypeStruct(array.shape,...  5.32 us

profile of v3, /device:TPU:1, one launch (start us, length us, event | category | flops | bytes accessed | tf_op | source)
XLA Modules:
  0.0 92.6 jit_solution(12507762927531376216)
XLA Ops:
  0.6 86.5 %step.1 = (bf16[256,768]{1,0:T(8,128)(2,1)}, bf16[256,768]{1,0:T(8,128)(2,1)}, bf16[2,2304,384]{2,1,0:T(8,128)(2,1)}, bf16[2,384,768]{2,1,0:T(8,128)(2,1)}, f32[...) custom-call(s32[2]{0:T(128)} %dilation.1, bf16[256,768]{1,0:T(8,128)(2,1)} %bitcast.12, s32[1,256]{1,0:T(1,128)} %tokens.1, ...), custom_call_target="tpu_custom_call" | custom-call | flops 10000000000 | bytes 20000000 | tf_op jit(solution)/shard_map/step/pallas_call | solution.py:603
  87.1 5.3 %widen.1 = (f32[4608,384]{1,0:T(8,128)}, f32[768,768]{1,0:T(8,128)}, bf16[256,768]{1,0:T(8,128)(2,1)}, bf16[256,768]{1,0:T(8,128)(2,1)}, f32[4,768]{1,0:T(4,128)}, /*index=5*/f32[2,768]{1,0:T(2,128)}, f32[2,384]{1,0:T(2,128)}) custom-call(bf16[4608,384]{1,0:T(8,128)(2,1)} %bitcast.8, bf16[768,768]{1,0:T(8,128)(2,1)} %bitcast.9, ...), custom_call_target="tpu_custom_call" | custom-call | flops 1000000 | bytes 15000000 | tf_op jit(solution)/shard_map/widen/pallas_call | solution.py:663

commit v4 on v3

--- a/solution.py
+++ b/solution.py
@@ -306,8 +306,8 @@
 
 def step_kernel(
     dilation, trunk, tokens, table, norm_gain, mid_gain, perm, cotangent, conv_hbm, out_hbm,
-    block_hbm, trunk_hbm, conv_grads, out_grads, table_grad, gain_grad, mid_grad,
-    block_out, table_pad, result, result_sem,
+    block_hbm, trunk_hbm, conv_grads, out_grads, table_hbm, gain_hbm, mid_hbm,
+    block_out, table_grad, gain_grad, mid_grad, table_pad, result, result_sem,
     conv_w, out_w, matrix, move, hidden, relabelled, u_pad, u_low, u_high, hat, slope, scale, mid,
     mid_hat, mid_slope, mid_scale, q, wide, back, rounded, e, dm_pad, dm_low, dm_high, grad, gain_acc, mid_acc,
     weight_sem, halo_send, halo_recv, grads, *scratch,
@@ -437,9 +437,12 @@
             else:
                 block_out[rows] = following
 
-        loop(OWN // TILE, join)
+        join(0)
+        join(OWN // TILE - 1)
         if b + 1 < LAYERS:
             pending = trade(b + 1, hidden.at[b + 1])
+        for i in range(1, OWN // TILE - 1):
+            join(i)
 
     leave(block_out, block_hbm)
     grad[...] = cotangent[...]
@@ -466,8 +469,11 @@
                 dm_pad[b, tile_at(i, DMAX), strand(s, MID)] = dm.astype(BF)
             mid_acc[b] += total
 
-        loop(OWN // TILE, middle_back)
+        middle_back(0)
+        middle_back(OWN // TILE - 1)
         pending = trade(LAYERS + b, dm_pad.at[b])
+        for i in range(1, OWN // TILE - 1):
+            middle_back(i)
         q_all = q[b].reshape(2 * OWN, MID)
         out_grad = dot_rows(q_all, e[...])
         sums[pl.ds(2304, MID)] = out_grad[:, :MID].astype(BF)
@@ -482,15 +488,18 @@
             wide[s] = dot_t(dm_pad[b, own, strand(s, MID)], conv_w[b, 1])
         if b == 0:
             totals[1].a_to_b()
+            totals[0].core_finish()
+            totals[0].a_start()
         for copy in pending:
             copy.wait()
         for s in range(2):
             dm_low[s] = dot(move[b, 1 - s], dm_pad[b, :, strand(s, MID)]).astype(BF)
             dm_high[s] = dot(move[b, s], dm_pad[b, :, strand(s, MID)]).astype(BF)
+        if b == 1:
+            totals[1].core_finish()
+            totals[1].a_start()
         for s in range(2):
             wide[s] += dot_t(dm_low[s], conv_w[b, 0]) + dot_t(dm_high[s], conv_w[b, 2])
-        totals[b].core_finish()
-        totals[b].a_start()
         if b == 0:
             totals[1].b_to_c()
 
@@ -551,6 +560,9 @@
         gain_grad[pl.ds(b, 1), pl.ds(0, MID)] = sums[8 + 2 * b:9 + 2 * b]
         gain_grad[pl.ds(b, 1), pl.ds(MID, MID)] = sums[9 + 2 * b:10 + 2 * b]
     mid_grad[...] = sums[12:14]
+    leave(table_grad, table_hbm)
+    leave(gain_grad, gain_hbm)
+    leave(mid_grad, mid_hbm)
     totals[0].forward()
     totals[0].finish()
     leave_sums(0)
@@ -564,9 +576,12 @@
     smem = pl.BlockSpec(memory_space=pltpu.SMEM)
     scratch = [
         pltpu.VMEM((OWN, CH), BF),
+        pltpu.VMEM((4, CH), F32),
+        pltpu.VMEM((LAYERS, CH), F32),
+        pltpu.VMEM((LAYERS, MID), F32),
         pltpu.VMEM((32, CH), F32),
         pltpu.VMEM((LAYERS, GROWS, LANES), BF),
-        pltpu.SemaphoreType.DMA((8,)),
+        pltpu.SemaphoreType.DMA((11,)),
         pltpu.VMEM((LAYERS, 3, CH, MID), BF),
         pltpu.VMEM((LAYERS, MID, CH), BF),
         pltpu.VMEM((CH, CH), BF),
@@ -612,7 +627,7 @@
             jax.ShapeDtypeStruct((LAYERS, MID), F32),
         ),
         in_specs=[smem] + [vmem] * 7 + [stay] * 2,
-        out_specs=(stay,) * 4 + (vmem,) * 3,
+        out_specs=(stay,) * 7,
         scratch_shapes=scratch + total_scratch() * 2 + small,
         compiler_params=pltpu.CompilerParams(collective_id=0, has_side_effects=True, vmem_limit_bytes=56 * 1024 * 1024),
         cost_estimate=pl.CostEstimate(flops=10**10, bytes_accessed=2 * 10**7, transcendentals=0),

time: 92.8 us -> 89.4 us (0.963)
  Pallas kernels: 91.8 us -> 88.5 us
    pallas_call x1, Pallas kernels: 86.5 us -> 83.2 us  [whole_step(): pl.pallas_call(step_kernel, out_shape=(jax.ShapeDtypeStruct((OWN, CH), BF...]
where the time goes in v4:
time: 89.4 us; the launch traced here: 89.3 us
  Pallas kernels  88.5 us (99%)
    pallas_call x1, Pallas kernels, whole_step(): pl.pallas_call(step_kernel, out_shape=(jax.ShapeDtypeStruct((OWN, CH), BF...  83.2 us
    pallas_call x1, Pallas kernels, widen(): pl.pallas_call(widen_kernel, out_shape=[jax.ShapeDtypeStruct(array.shape,...  5.32 us

profile of v4, /device:TPU:1, one launch (start us, length us, event | category | flops | bytes accessed | tf_op | source)
XLA Modules:
  0.0 89.3 jit_solution(6446854138643080903)
XLA Ops:
  0.6 83.2 %step.1 = (bf16[256,768]{1,0:T(8,128)(2,1)}, bf16[256,768]{1,0:T(8,128)(2,1)}, bf16[2,2304,384]{2,1,0:T(8,128)(2,1)}, bf16[2,384,768]{2,1,0:T(8,128)(2,1)}, f32[...) custom-call(s32[2]{0:T(128)} %dilation.1, bf16[256,768]{1,0:T(8,128)(2,1)} %bitcast.12, s32[1,256]{1,0:T(1,128)} %tokens.1, ...), custom_call_target="tpu_custom_call" | custom-call | flops 10000000000 | bytes 20000000 | tf_op jit(solution)/shard_map/step/pallas_call | solution.py:618
  83.8 5.3 %widen.1 = (f32[4608,384]{1,0:T(8,128)}, f32[768,768]{1,0:T(8,128)}, bf16[256,768]{1,0:T(8,128)(2,1)}, bf16[256,768]{1,0:T(8,128)(2,1)}, f32[4,768]{1,0:T(4,128)}, /*index=5*/f32[2,768]{1,0:T(2,128)}, f32[2,384]{1,0:T(2,128)}) custom-call(bf16[4608,384]{1,0:T(8,128)(2,1)} %bitcast.8, bf16[768,768]{1,0:T(8,128)(2,1)} %bitcast.9, ...), custom_call_target="tpu_custom_call" | custom-call | flops 1000000 | bytes 15000000 | tf_op jit(solution)/shard_map/widen/pallas_call | solution.py:678

commit v5 on v4

--- a/solution.py
+++ b/solution.py
@@ -268,7 +268,7 @@
         body(index)
         return carry
 
-    lax.fori_loop(0, count, step, 0, unroll=2 if count % 2 == 0 else 1)
+    lax.fori_loop(0, count, step, 0, unroll=4 if count % 4 == 0 else 1)
 
 
 def tile_at(index, base=0, size=TILE):

time: 89.4 us -> 88.3 us (0.988)
  Pallas kernels: 88.5 us -> 87.3 us
    pallas_call x1, Pallas kernels: 83.2 us -> 82 us  [whole_step(): pl.pallas_call(step_kernel, out_shape=(jax.ShapeDtypeStruct((OWN, CH), BF...]
where the time goes in v5:
time: 88.3 us; the launch traced here: 88.2 us
  Pallas kernels  87.3 us (99%)
    pallas_call x1, Pallas kernels, whole_step(): pl.pallas_call(step_kernel, out_shape=(jax.ShapeDtypeStruct((OWN, CH), BF...  82 us
    pallas_call x1, Pallas kernels, widen(): pl.pallas_call(widen_kernel, out_shape=[jax.ShapeDtypeStruct(array.shape,...  5.32 us

profile of v5, /device:TPU:1, one launch (start us, length us, event | category | flops | bytes accessed | tf_op | source)
XLA Modules:
  0.0 88.2 jit_solution(3477065459645189220)
XLA Ops:
  0.6 82.0 %step.1 = (bf16[256,768]{1,0:T(8,128)(2,1)}, bf16[256,768]{1,0:T(8,128)(2,1)}, bf16[2,2304,384]{2,1,0:T(8,128)(2,1)}, bf16[2,384,768]{2,1,0:T(8,128)(2,1)}, f32[...) custom-call(s32[2]{0:T(128)} %dilation.1, bf16[256,768]{1,0:T(8,128)(2,1)} %bitcast.12, s32[1,256]{1,0:T(1,128)} %tokens.1, ...), custom_call_target="tpu_custom_call" | custom-call | flops 10000000000 | bytes 20000000 | tf_op jit(solution)/shard_map/step/pallas_call | solution.py:618
  82.7 5.3 %widen.1 = (f32[4608,384]{1,0:T(8,128)}, f32[768,768]{1,0:T(8,128)}, bf16[256,768]{1,0:T(8,128)(2,1)}, bf16[256,768]{1,0:T(8,128)(2,1)}, f32[4,768]{1,0:T(4,128)}, /*index=5*/f32[2,768]{1,0:T(2,128)}, f32[2,384]{1,0:T(2,128)}) custom-call(bf16[4608,384]{1,0:T(8,128)(2,1)} %bitcast.8, bf16[768,768]{1,0:T(8,128)(2,1)} %bitcast.9, ...), custom_call_target="tpu_custom_call" | custom-call | flops 1000000 | bytes 15000000 | tf_op jit(solution)/shard_map/widen/pallas_call | solution.py:678
